TPU v7x, 32 devices: a whole 2x2x4 slice. The times are simulated.
32 devices in a mesh: grp: 2 (over y), row: 4 (over z), col: 2 (over x), sub: 2 (over core).
Axes of the slice: x: 2, y: 2, z: 4, core: 2. Of those that a mesh axis runs over, the one named last changes fastest.
Arguments:
- samples: bfloat16 [512, 2, 16, 512], P(('grp', 'row', 'col', 'sub')), parts along dimension 0, may hold values from -6 to 6
- analysis_taps: float32 [16, 16], replicated, may hold values from -1 to 1
- synthesis_taps: float32 [16, 16], replicated, may hold values from -1 to 1
- antenna_station: int32 [512], P('grp'), parts along dimension 0, may hold values from 0 to 31, as said below
- station_group: int32 [64, 1], P('grp'), parts along dimension 0, may hold values from 0 to 7
- beam_group: int32 [2048], P('grp'), parts along dimension 0, may hold values from 0 to 7
- beam_weights: bfloat16 [32, 2, 1024, 32], P(('grp', 'row'), None, ('col', 'sub')), parts along dimension 0, may hold values from -6 to 6
Outputs:
- visibilities: float32 [16, 2, 64, 32], P('row', None, ('grp', 'col', 'sub')), parts along dimension 2
- beam_series: float32 [2048, 2, 16, 512], P(('grp', 'col', 'sub', 'row')), parts along dimension 0
There are 2 independent parts, one for each index of `grp`. A program takes and returns all parts, laid end to end along the dimension named above; an argument that names none is the same for every part. Nothing has to cross between parts.
Inputs may be any that keep to these rules, and one draw needn't show every extreme that they name: `antenna_station`: every station is named by exactly 8 antennas.
All inputs are finite; a program needn't handle non-finite values.
Results may differ from a plain program's by a relative error of at most 0.005.
Values may be sent and summed in bfloat16 or wider, within the bound.
A program may use at most 64 MiB of HBM per device.

v0:
```python
import math

import jax
import jax.numpy as jnp
from jax import lax
from jax.sharding import PartitionSpec as P

ANTENNAS_PER_STN = 8
SPEC = 512


def polyphase(signal, coefficients):
    length = signal.shape[-1]
    output = coefficients[0][:, None] * signal
    for tap_index in range(1, coefficients.shape[0]):
        shifted = jnp.pad(
            signal[..., : length - tap_index], [(0, 0)] * (signal.ndim - 1) + [(tap_index, 0)]
        )
        output = output + coefficients[tap_index][:, None] * shifted
    return output


def fourier_table(length, direction):
    indices = jnp.arange(length)
    angles = (
        2.0 * math.pi / length * (indices[:, None] * indices[None, :] % length).astype(jnp.float32)
    )
    cosine_part = jnp.cos(angles)
    sine_part = jnp.sin(angles)
    table = jnp.stack(
        [
            jnp.stack([cosine_part, direction * sine_part]),
            jnp.stack([-direction * sine_part, cosine_part]),
        ]
    )
    return table.transpose(0, 2, 1, 3) * (1.0 / math.sqrt(length))


def body(
    samples, analysis_taps, synthesis_taps, antenna_station, station_group, beam_group, beam_weights
):
    high = lax.Precision.HIGHEST
    block_count = lax.axis_size(("col", "sub"))
    block_index = lax.axis_index(("col", "sub"))
    filtered = polyphase(samples.astype(jnp.float32), analysis_taps)
    spectra = jnp.einsum(
        "aqcf,qcpk->apkf", filtered, fourier_table(samples.shape[2], -1.0), precision=high
    ).astype(jnp.bfloat16)
    turned = lax.all_to_all(spectra, "row", split_axis=2, concat_axis=0, tiled=True)
    local_count = spectra.shape[0]
    held_rows = turned.shape[0]
    chan_rows = turned.shape[2]
    spec_len = turned.shape[3]
    station_count = station_group.shape[0]
    flat_width = 2 * chan_rows * spec_len
    tile_rows = station_count // block_count
    shard_rows = lax.all_gather(turned, ("col", "sub"), axis=0, tiled=True)
    row_total = shard_rows.shape[0]
    positions = jnp.arange(row_total, dtype=jnp.int32)
    source_block = positions // held_rows
    offset_rows = positions % held_rows
    source_row = offset_rows // local_count
    antenna = offset_rows % local_count
    global_index = (source_row * block_count + source_block) * local_count + antenna
    targets = antenna_station[global_index]
    wanted = jnp.arange(station_count, dtype=jnp.int32)
    one_hot = (targets[None, :] == wanted[:, None]).astype(jnp.bfloat16)
    summed_values = jnp.dot(
        one_hot, shard_rows.reshape(row_total, flat_width), preferred_element_type=jnp.float32
    )
    flat_stations = (summed_values * (1.0 / math.sqrt(ANTENNAS_PER_STN))).astype(jnp.bfloat16)
    station_list = flat_stations.reshape(station_count, 2, chan_rows, spec_len)
    real_part = station_list[:, 0]
    imag_part = station_list[:, 1]
    own_rows = lax.dynamic_slice_in_dim(station_list, block_index * tile_rows, tile_rows, 0)
    own_real = own_rows[:, 0]
    own_imag = own_rows[:, 1]
    vis_real = (
        jnp.einsum("icf,jcf->cij", own_real, real_part, preferred_element_type=jnp.float32)
        + jnp.einsum("icf,jcf->cij", own_imag, imag_part, preferred_element_type=jnp.float32)
    ) * (1.0 / SPEC)
    vis_imag = (
        jnp.einsum("icf,jcf->cij", own_imag, real_part, preferred_element_type=jnp.float32)
        - jnp.einsum("icf,jcf->cij", own_real, imag_part, preferred_element_type=jnp.float32)
    ) * (1.0 / SPEC)
    visibilities = jnp.stack([vis_real, vis_imag], axis=1)
    beam_block = beam_weights.shape[2]
    own_groups = lax.dynamic_slice_in_dim(beam_group, block_index * beam_block, beam_block, 0)
    members = station_group[:, 0][None, :] == own_groups[:, None]
    scaling = 1.0 / jnp.sqrt(jnp.sum(members.astype(jnp.float32), axis=1))
    weights = jnp.where(members[None, None], beam_weights, jnp.zeros((), jnp.bfloat16))
    weight_real = weights[:, 0]
    imaginary_weight = weights[:, 1]
    beam_real = jnp.einsum(
        "cbs,scf->bcf", weight_real, real_part, preferred_element_type=jnp.float32
    ) - jnp.einsum("cbs,scf->bcf", imaginary_weight, imag_part, preferred_element_type=jnp.float32)
    beam_imag = jnp.einsum(
        "cbs,scf->bcf", weight_real, imag_part, preferred_element_type=jnp.float32
    ) + jnp.einsum("cbs,scf->bcf", imaginary_weight, real_part, preferred_element_type=jnp.float32)
    beams = (jnp.stack([beam_real, beam_imag], axis=1) * scaling[:, None, None, None]).astype(
        jnp.bfloat16
    )
    returned = lax.all_to_all(beams, "row", split_axis=0, concat_axis=2, tiled=True)
    inverse = jnp.einsum(
        "bqkf,qkpc->bpcf",
        returned.astype(jnp.float32),
        fourier_table(returned.shape[2], 1.0),
        precision=high,
    )
    beam_series = polyphase(inverse, synthesis_taps)
    return (visibilities, beam_series)


def solution(mesh):
    return jax.shard_map(
        body,
        mesh=mesh,
        in_specs=(
            P(("grp", "row", "col", "sub"), None, None, None),
            P(),
            P(),
            P("grp"),
            P("grp", None),
            P("grp"),
            P(("grp", "row"), None, ("col", "sub"), None),
        ),
        out_specs=(
            P("row", None, ("grp", "col", "sub"), None),
            P(("grp", "col", "sub", "row"), None, None, None),
        ),
        check_vma=False,
    )
```

profile of v0, /device:TPU:0, one launch (start us, length us, event | category | flops | bytes accessed | tf_op | source)
XLA Modules:
  0.0 157.8 jit_solution(14489460331540854039)
XLA Ops:
  7.4 1.2 slice.274
  8.5 1.2 slice.275
  11.4 0.2 copy-done.3
  11.6 5.1 %fusion.3 = bf16[16,2,16,512]{3,2,0,1:T(8,128)(2,1)S(1)} fusion(f32[16,2,16,497]{3,2,1,0:T(8,128)S(1)} %slice.288, f32[16,2,16,498]{3,2,1,0:T(8,128)S(1)} %slice.287, f32[16,2,16,499]{3,2,1,0:T(8,128)S(1)} %slice.286, f32[16,2,16,500]{3,2,1,0:T(8,128)S(1)} %slice.285, f32[16,2,16,501]{3,2,1,0:T(8,128)S(1)} %slice.284, f32[16,2,16,502]{3,2,1,0:T(8,128)S(1)} %slice.283, ...), kind=kOutput, calls=%fused_computation.11 | convolution fusion | flops 109316096 | bytes 16536576 | tf_op jit(solution)/shard_map/aqcf,qcpk->apkf/dot_general | solution.py:46
  16.8 0.3 copy.55
  17.1 20.6 %all_to_all.36 = bf16[16,2,16,512]{3,0,1,2:T(8,128)(2,1)S(1)} all-to-all(bf16[16,2,16,512]{3,0,1,2:T(8,128)(2,1)S(1)} %copy.55), channel_id=1, replica_groups=mesh['grp'=2,'row'=4,'col'=2,'sub'=2] {'row'}, dimensions={2} | all-to-all | bytes 1048576 | tf_op jit(solution)/shard_map/all_to_all | solution.py:49
  37.7 0.8 copy.57
  38.5 0.8 dynamic_slice.7
  39.4 1.9 %gather_fusion = s32[256]{0:T(256)S(1)} fusion(s32[256]{0:T(256)S(1)} %copy-done, s32[1024]{0:T(1024)S(1)} %pad_clamp_fusion), kind=kCustom, calls=%fused_computation | custom fusion | bytes 3072 | tf_op jit(solution)/shard_map/gather | solution.py:65
  41.5 18.9 %all-gather.2.cloned.1.call-done = bf16[256,2,4,512]{3,0,2,1:T(8,128)(2,1)} async-done(((bf16[64,2,4,512]{3,0,2,1:T(8,128)(2,1)}), bf16[256,2,4,512]{3,0,2,1:T(8,128)(2,1)}) %all-gather.2.cloned.1.call-update) | async-done | bytes 2097168 | tf_op jit(solution)/shard_map/all_gather | solution.py:57
  60.4 2.8 %copy.58 = bf16[256,2,4,512]{0,3,2,1:T(8,128)(2,1)S(1)} copy(bf16[256,2,4,512]{3,0,2,1:T(8,128)(2,1)} %all-gather.2.cloned.1.call-done) | data formatting | bytes 4194304 | tf_op jit(solution)/shard_map/all_gather | solution.py:57
  63.2 0.7 fusion
  63.9 0.2 reshape.289
  64.2 0.5 fusion.72
  64.6 0.5 fusion.75
  65.1 0.5 subtract_bitcast_fusion
  65.6 0.5 add_bitcast_fusion
  66.1 0.4 fusion.1
  66.6 3.1 %copy.64 = bf16[256,2,4,512]{3,2,1,0:T(4,128)(2,1)} copy(bf16[256,2,4,512]{0,3,2,1:T(8,128)(2,1)S(1)} %fusion.1) | data formatting | bytes 4194304 | tf_op jit(solution)/shard_map/convert_element_type | solution.py:100
  69.6 4.6 %all-to-all-start.1 = ((bf16[256,2,4,512]{3,2,1,0:T(4,128)(2,1)}), bf16[256,2,4,512]{3,2,1,0:T(4,128)(2,1)S(1)}, u32[]{:S(2)}, u32[]{:S(2)}) async-start(bf16[256,2,4,512]{3,2,1,0:T(4,128)(2,1)} %copy.64), calls=%async_computation.1 | async-start | bytes 4194304 | tf_op jit(solution)/shard_map/all_to_all | solution.py:103
  74.3 0.1 fusion.74
  74.5 0.2 fusion.7
  74.6 0.1 fusion.73
  74.8 0.2 fusion.5
  74.9 0.6 copy.67
  75.6 47.3 %all-to-all-done.1 = bf16[256,2,4,512]{3,2,1,0:T(4,128)(2,1)S(1)} async-done(((bf16[256,2,4,512]{3,2,1,0:T(4,128)(2,1)}), bf16[256,2,4,512]{3,2,1,0:T(4,128)(2,1)S(1)}, u32[]{:S(2)}, u32[]{:S(2)}) %all-to-all-start.1) | async-done | bytes 2097184 | tf_op jit(solution)/shard_map/all_to_all | solution.py:103
  122.8 0.7 copy.65
  123.5 2.9 %copy.66 = bf16[64,2,4,4,512]{4,3,2,1,0:T(4,128)(2,1)} copy(bf16[64,2,4,4,512]{4,0,2,3,1:T(8,128)(2,1)S(1)} %bitcast.188) | data formatting | bytes 4194304 | tf_op jit(solution)/shard_map/all_to_all | solution.py:103
  126.5 2.5 %reshape.302 = bf16[64,2,16,512,1]{3,2,1,0,4:T(8,128)(2,1)S(1)} reshape(bf16[64,2,4,4,512]{4,3,2,1,0:T(4,128)(2,1)} %copy.66) | data formatting | bytes 4194304 | tf_op jit(solution)/shard_map/all_to_all | solution.py:103
  129.0 2.0 %convolution_bitcast_fusion = f32[64,2,16,512]{3,2,0,1:T(8,128)S(1)} fusion(bf16[64,2,16,512,1]{3,2,1,0,4:T(8,128)(2,1)S(1)} %reshape.302, f32[1,2,16,16]{2,3,0,1:T(8,128)S(1)} %get-tuple-element.37, f32[1,2,16,16]{2,3,0,1:T(8,128)S(1)} %get-tuple-element.16), kind=kOutput, calls=%fused_computation.6 | convolution fusion | flops 402655232 | bytes 6295552 | tf_op jit(solution)/shard_map/bqkf,qkpc->bpcf/dot_general | solution.py:104
  131.0 17.3 %multiply_add_fusion = f32[64,2,16,512]{3,2,0,1:T(8,128)S(1)} fusion(f32[64,2,16,497]{3,2,0,1:T(8,128)S(1)} %bitcast.172, f32[64,2,16,498]{3,2,0,1:T(8,128)S(1)} %bitcast.173, f32[64,2,16,499]{3,2,0,1:T(8,128)S(1)} %bitcast.174, f32[64,2,16,500]{3,2,0,1:T(8,128)S(1)} %bitcast.175, f32[64,2,16,501]{3,2,0,1:T(8,128)S(1)} %bitcast.176, ...), kind=kLoop, calls=%fused_computation.5 | loop fusion | flops 32505856 | bytes 70321152 | tf_op jit(solution)/shard_map/add | solution.py:19
  148.4 2.6 %copy.68 = f32[64,2,16,512]{3,2,1,0:T(8,128)} copy(f32[64,2,16,512]{3,2,0,1:T(8,128)S(1)} %multiply_add_fusion) | data formatting | bytes 8388608
  (40 shorter events, 2.2 us)
Async XLA Ops:
  7.2 32.3 %copy-start = (s32[256]{0:T(256)S(1)}, s32[256]{0:T(256)}, u32[]{:S(2)}) copy-start(s32[256]{0:T(256)} %param.10) | copy-start | bytes 3076
  7.2 2.5 %copy-start.1 = (bf16[16,2,16,512]{3,2,1,0:T(8,128)(2,1)S(1)}, bf16[16,2,16,512]{3,2,1,0:T(8,128)(2,1)}, u32[]{:S(2)}) copy-start(bf16[16,2,16,512]{3,2,1,0:T(8,128)(2,1)} %param.7) | copy-start | bytes 1572868
  7.2 53.2 %all-gather.2.cloned.1.call-start = ((), (), s32[]{:S(2)}) async-start(), calls=%async_computation.2 | async-start | bytes 2621440 | tf_op jit(solution)/shard_map/all_gather | solution.py:57
  10.9 0.7 copy-start.3
  11.6 27.7 %copy-start.5 = (s32[32,1]{0,1:T(1,128)S(1)}, s32[32,1]{0,1:T(1,128)}, u32[]{:S(2)}) copy-start(s32[32,1]{0,1:T(1,128)} %param.11) | copy-start | bytes 388
  16.7 24.7 %copy-start.2 = (bf16[4,2,256,32]{2,3,1,0:T(8,128)(2,1)S(1)}, bf16[4,2,256,32]{2,3,1,0:T(8,128)(2,1)}, u32[]{:S(2)}) copy-start(bf16[4,2,256,32]{2,3,1,0:T(8,128)(2,1)} %param.13) | copy-start | bytes 393220
  66.5 7.7 %copy-start.4 = (f32[16,16]{1,0:T(8,128)S(1)}, f32[16,16]{1,0:T(8,128)}, u32[]{:S(2)}) copy-start(f32[16,16]{1,0:T(8,128)} %param.9) | copy-start | bytes 3076
  69.6 53.2 %all-to-all-start.1 = ((bf16[256,2,4,512]{3,2,1,0:T(4,128)(2,1)}), bf16[256,2,4,512]{3,2,1,0:T(4,128)(2,1)S(1)}, u32[]{:S(2)}, u32[]{:S(2)}) async-start(bf16[256,2,4,512]{3,2,1,0:T(4,128)(2,1)} %copy.64), calls=%async_computation.1 | async-start | bytes 4194304 | tf_op jit(solution)/shard_map/all_to_all | solution.py:103
Sparse Core Ops, SparseCore 0:
  38.6 21.6 all-gather.1
where the time goes:
time: 158 us
  waiting for transfers between devices  66.2 us (42%)
  local copies, waits for them, and re-layouts  23.5 us (15%)
  blocking collectives  20.6 us (13%)
  other arithmetic  18.1 us (11%)
  between operations  14.4 us (9%)
  matrix products  10.3 us (7%)
  starting transfers between devices  4.66 us (3%)
    all_to_all x1, waiting for transfers between devices, body(): lax.all_to_all(beams, 'row', split_axis=0, concat_axis=2, tiled=True)  47.3 us
    all_to_all x1, blocking collectives, body(): lax.all_to_all(spectra, 'row', split_axis=2, concat_axis=0, tiled=True)  20.6 us
    all_gather x1, waiting for transfers between devices, body(): shard_rows = lax.all_gather(turned, ('col', 'sub'), axis=0, tiled=True)  18.9 us
    add x1, other arithmetic, polyphase(): output = output + coefficients[tap_index][:, None] * shifted  17.3 us
    all_to_all x3, local copies, waits for them, and re-layouts, body(): lax.all_to_all(beams, 'row', split_axis=0, concat_axis=2, tiled=True)  6.19 us
    dot_general x1, matrix products, body(): jnp.einsum('aqcf,qcpk->apkf', filtered, fourier_table(samples.shape[2], -...  5.12 us
    all_to_all x1, starting transfers between devices, body(): lax.all_to_all(beams, 'row', split_axis=0, concat_axis=2, tiled=True)  4.62 us
    slice x15, local copies, waits for them, and re-layouts, polyphase(): signal[..., :length - tap_index]  3.91 us
  transfers between devices with their start and end apart: 2, of which 2 were waited for; matrix products, arithmetic and copies ran while one was open for 3% of the time, Pallas kernels for 0%

commit v1 on v0

--- a/solution.py
+++ b/solution.py
@@ -1,9 +1,15 @@
+import functools
 import math
 
 import jax
 import jax.numpy as jnp
+import numpy as np
 from jax import lax
+from jax.experimental import pallas as pl
+from jax.experimental.pallas import tpu as pltpu
 from jax.sharding import PartitionSpec as P
+
+MESH = pl.DeviceIdType.MESH
 
 ANTENNAS_PER_STN = 8
 SPEC = 512
@@ -111,9 +117,371 @@
     return (visibilities, beam_series)
 
 
+def exchange_kernel(
+    n_row, n_col, n_sub,
+    x_ref, w_ref, station_ref, taps_ref,
+    lanes_ref, w_out_ref,
+    recv, own_sem, send_sem, recv_sem, w_send, w_recv, g_send, g_recv,
+):
+    n = n_row * n_col * n_sub
+    row, col, sub = lax.axis_index("row"), lax.axis_index("col"), lax.axis_index("sub")
+    me = (row * n_col + col) * n_sub + sub
+
+    def coords(index):
+        return {
+            "row": lax.div(index, n_col * n_sub),
+            "col": lax.rem(lax.div(index, n_sub), n_col),
+            "sub": lax.rem(index, n_sub),
+        }
+
+    barrier = pltpu.get_barrier_semaphore()
+
+    def greet(step, carry):
+        pl.semaphore_signal(
+            barrier, inc=1, device_id=coords(lax.rem(me + step, n)), device_id_type=MESH
+        )
+        return carry
+
+    lax.fori_loop(1, n, greet, 0)
+    own = pltpu.make_async_copy(x_ref.at[me], recv.at[me], own_sem.at[0])
+    own.start()
+    own_w = pltpu.make_async_copy(w_ref.at[row], w_out_ref.at[row], own_sem.at[1])
+    own_w.start()
+    pl.semaphore_wait(barrier, n - 1)
+
+    def slab(step):
+        peer = lax.rem(me + step, n)
+        return pltpu.make_async_remote_copy(
+            src_ref=x_ref.at[peer], dst_ref=recv.at[me],
+            send_sem=send_sem.at[step], recv_sem=recv_sem.at[step],
+            device_id=coords(peer), device_id_type=MESH,
+        )
+
+    def weight(step):
+        peer = lax.rem(row + step, n_row)
+        return pltpu.make_async_remote_copy(
+            src_ref=w_ref.at[peer], dst_ref=w_out_ref.at[row],
+            send_sem=w_send.at[step], recv_sem=w_recv.at[step],
+            device_id={"row": peer, "col": col, "sub": sub}, device_id_type=MESH,
+        )
+
+    def start_slab(step, carry):
+        slab(step).start()
+        return carry
+
+    lax.fori_loop(1, n, start_slab, 0)
+    for step in range(1, n_row):
+        weight(step).start()
+
+    stations2, width = lanes_ref.shape[1], lanes_ref.shape[2]
+    stations = stations2 // 2
+    per = x_ref.shape[1]
+    total = n * per
+    place = lax.broadcasted_iota(jnp.int32, (stations2, total), 0)
+    column = lax.broadcasted_iota(jnp.int32, (stations2, total), 1)
+    part = lax.rem(lax.div(column, per // 2), 2)
+    wanted = station_ref[...] + part * stations
+    one_hot = jnp.where(place == wanted, 1.0, 0.0).astype(jnp.bfloat16)
+
+    own.wait()
+
+    def finish_slab(step, carry):
+        slab(step).wait_recv()
+        return carry
+
+    lax.fori_loop(1, n, finish_slab, 0)
+    summed = jnp.dot(
+        one_hot, recv[...].reshape(total, width), preferred_element_type=jnp.float32
+    )
+    frame = lax.broadcasted_iota(jnp.int32, summed.shape, 1)
+    filtered = taps_ref[0, me] * summed
+    for tap in range(1, taps_ref.shape[0]):
+        moved = jnp.where(frame >= tap, pltpu.roll(summed, tap, 1), 0.0)
+        filtered = filtered + taps_ref[tap, me] * moved
+    scale = 1.0 / math.sqrt(ANTENNAS_PER_STN * n)
+    lanes_ref[me] = (filtered * scale).astype(jnp.bfloat16)
+
+    def forward(lane, slot, target):
+        return pltpu.make_async_remote_copy(
+            src_ref=lanes_ref.at[lane], dst_ref=lanes_ref.at[lane],
+            send_sem=g_send.at[slot], recv_sem=g_recv.at[lane],
+            device_id=target, device_id_type=MESH,
+        )
+
+    def lane_of(r, c, s):
+        return (r * n_col + c) * n_sub + s
+
+    other_col = {"row": row, "col": 1 - col, "sub": sub}
+    other_sub = {"row": row, "col": col, "sub": 1 - sub}
+    sends = []
+
+    def send(lane, target):
+        copy = forward(lane, len(sends), target)
+        copy.start()
+        sends.append(copy)
+
+    def arrived(lane):
+        forward(lane, 0, other_sub).wait_recv()
+
+    for step in range(1, n_row):
+        send(me, {"row": lax.rem(row + step, n_row), "col": col, "sub": sub})
+    send(me, other_col)
+    send(me, other_sub)
+    for step in range(1, n_row):
+        lane = lane_of(lax.rem(row + n_row - step, n_row), col, sub)
+        arrived(lane)
+        send(lane, other_col)
+        send(lane, other_sub)
+    for step in range(n_row):
+        lane = lane_of(lax.rem(row + n_row - step, n_row), 1 - col, sub)
+        arrived(lane)
+        send(lane, other_sub)
+    for step in range(n_row):
+        for c in range(n_col):
+            arrived(lane_of(lax.rem(row + n_row - step, n_row), c, 1 - sub))
+    for copy in sends:
+        copy.wait_send()
+
+    def finish_send(step, carry):
+        slab(step).wait_send()
+        return carry
+
+    lax.fori_loop(1, n, finish_send, 0)
+    own_w.wait()
+    for step in range(1, n_row):
+        weight(step).wait()
+
+
+def exchange(x, w, station_row, taps, n_row, n_col, n_sub):
+    n = n_row * n_col * n_sub
+    stations2 = station_row[1]
+    any_space = pl.BlockSpec(memory_space=pl.ANY)
+    vmem = pl.BlockSpec(memory_space=pltpu.VMEM)
+    width = x.shape[2]
+    dma = pltpu.SemaphoreType.DMA
+    sends = (n_row - 1) * 3 + 2 + n_row
+    return pl.pallas_call(
+        functools.partial(exchange_kernel, n_row, n_col, n_sub),
+        out_shape=(
+            jax.ShapeDtypeStruct((n, stations2, width), jnp.bfloat16),
+            jax.ShapeDtypeStruct(w.shape, jnp.bfloat16),
+        ),
+        in_specs=[any_space, any_space, vmem, pl.BlockSpec(memory_space=pltpu.SMEM)],
+        out_specs=(vmem, vmem),
+        scratch_shapes=[
+            pltpu.VMEM((n, x.shape[1], width), jnp.bfloat16),
+            dma((2,)), dma((n,)), dma((n,)), dma((n_row,)), dma((n_row,)),
+            dma((sends,)), dma((n,)),
+        ],
+        compiler_params=pltpu.CompilerParams(
+            collective_id=0, has_side_effects=True, vmem_limit_bytes=32 * 1024 * 1024
+        ),
+        name="exchange",
+    )(x, w, station_row[0], taps)
+
+
+def fourier(points):
+    count = len(points)
+    if count == 1:
+        return points
+    even, odd = fourier(points[0::2]), fourier(points[1::2])
+    half = count // 2
+    low, high = [], []
+    for index in range(half):
+        (er, ei), (r, i) = even[index], odd[index]
+        if index == 0:
+            tr, ti = r, i
+        elif 4 * index == count:
+            tr, ti = i, -r
+        else:
+            c, s = math.cos(2 * math.pi * index / count), math.sin(2 * math.pi * index / count)
+            if 8 * index == count:
+                tr, ti = (r + i) * c, (i - r) * c
+            elif 8 * index == 3 * count:
+                tr, ti = (i - r) * s, -(r + i) * s
+            else:
+                tr, ti = r * c + i * s, i * c - r * s
+        low.append((er + tr, ei + ti))
+        high.append((er - tr, ei - ti))
+    return low + high
+
+
+def beam_kernel(
+    lanes_ref, w_ref, sgroup_ref, bgroup_ref, cos_ref, sin_ref, taps_ref,
+    vis_ref, out_ref, spectra, gram, inverse,
+):
+    chan, stations2, width = lanes_ref.shape
+    stations = stations2 // 2
+
+    @pl.when(pl.program_id(0) == 0)
+    def _():
+        step_rows = 16
+
+        @pl.loop(0, stations // step_rows)
+        def _(block):
+            low = pl.multiple_of(block * step_rows, step_rows)
+            for start in range(0, width, 128):
+                points = [
+                    (
+                        lanes_ref[c, pl.ds(low, step_rows), start : start + 128].astype(jnp.float32),
+                        lanes_ref[c, pl.ds(low + stations, step_rows), start : start + 128].astype(
+                            jnp.float32
+                        ),
+                    )
+                    for c in range(chan)
+                ]
+                for k, (re, im) in enumerate(fourier(points)):
+                    spectra[k, pl.ds(low, step_rows), start : start + 128] = re.astype(jnp.bfloat16)
+                    spectra[k, pl.ds(low + stations, step_rows), start : start + 128] = im.astype(
+                        jnp.bfloat16
+                    )
+
+        chan_rows, _, own, _ = vis_ref.shape
+        first = lax.axis_index("row") * chan_rows
+        block_index = lax.axis_index(("col", "sub"))
+        begin = pl.multiple_of(block_index * own, own)
+        for k in range(chan_rows):
+            block = spectra[first + k]
+            gram[...] = lax.dot_general(
+                block, block, (((1,), (1,)), ((), ())), preferred_element_type=jnp.float32
+            )
+            top = gram[pl.ds(begin, own), :]
+            bottom = gram[pl.ds(begin + stations, own), :]
+            vis_ref[k, 0] = (top[:, :stations] + bottom[:, stations:]) * (1.0 / width)
+            vis_ref[k, 1] = (bottom[:, :stations] - top[:, stations:]) * (1.0 / width)
+
+    rows = bgroup_ref.shape[0]
+    total = chan * stations2
+    weight = jnp.concatenate([w_ref[r] for r in range(w_ref.shape[0])], axis=1).astype(jnp.float32)
+    members = sgroup_ref[...] == bgroup_ref[...]
+    count = jnp.sum(members.astype(jnp.float32), axis=1, keepdims=True) * (1.0 / (2 * chan))
+    weight = jnp.where(members, weight, 0.0) * (1.0 / jnp.sqrt(count))
+    position = lax.broadcasted_iota(jnp.int32, (rows, total), 1)
+    first_half = lax.rem(position, stations2) < stations
+    plain = jnp.where(first_half, weight, -weight)
+    swapped = jnp.where(
+        first_half, pltpu.roll(weight, total - stations, 1), pltpu.roll(weight, stations, 1)
+    )
+    cos_table, sin_table = cos_ref[...], sin_ref[...]
+    matrix = []
+    for b in range(rows):
+        a0, a1 = plain[b : b + 1], swapped[b : b + 1]
+        matrix.append((cos_table * a0 - sin_table * a1).astype(jnp.bfloat16))
+        matrix.append((cos_table * a1 + sin_table * a0).astype(jnp.bfloat16))
+    inverse[...] = jnp.dot(
+        jnp.concatenate(matrix, axis=0),
+        spectra[...].reshape(total, width),
+        preferred_element_type=jnp.float32,
+    )
+    lane = lax.broadcasted_iota(jnp.int32, (chan, 128), 1)
+
+    def shift(tiles, amount):
+        turned = [pltpu.roll(tile, amount, 1) for tile in tiles]
+        before = [jnp.zeros_like(turned[0])] + turned[:-1]
+        return [jnp.where(lane >= amount, t, b) for t, b in zip(turned, before)]
+
+    taps = taps_ref.shape[0]
+    stride = 4
+    for index in range(2 * rows):
+        tiles = [
+            inverse[index * chan : (index + 1) * chan, start : start + 128]
+            for start in range(0, width, 128)
+        ]
+        moved = [tiles]
+        for amount in range(1, stride):
+            moved.append(shift(tiles, amount))
+        total_tiles = None
+        for high in range(taps // stride - 1, -1, -1):
+            if total_tiles is not None:
+                total_tiles = shift(total_tiles, stride)
+            for low in range(stride):
+                tap = taps_ref[high * stride + low]
+                terms = [tap * tile for tile in moved[low]]
+                total_tiles = (
+                    terms if total_tiles is None else [a + t for a, t in zip(total_tiles, terms)]
+                )
+        for number, tile in enumerate(total_tiles):
+            out_ref[index // 2, index % 2, :, number * 128 : (number + 1) * 128] = tile
+
+
+def beamform(lanes, w, sgroup, bgroup, cos_table, sin_table, taps, vis_shape, rows):
+    chan, stations2, width = lanes.shape
+    beams = bgroup.shape[0]
+    whole = lambda *shape: pl.BlockSpec(shape, lambda i: (0,) * len(shape))
+    return pl.pallas_call(
+        beam_kernel,
+        grid=(beams // rows,),
+        out_shape=(
+            jax.ShapeDtypeStruct(vis_shape, jnp.float32),
+            jax.ShapeDtypeStruct((beams, 2, chan, width), jnp.float32),
+        ),
+        in_specs=[
+            whole(*lanes.shape),
+            pl.BlockSpec((w.shape[0], rows, w.shape[2]), lambda i: (0, i, 0)),
+            whole(*sgroup.shape),
+            pl.BlockSpec((rows, 1), lambda i: (i, 0)),
+            whole(*cos_table.shape),
+            whole(*sin_table.shape),
+            whole(*taps.shape),
+        ],
+        out_specs=(
+            whole(*vis_shape),
+            pl.BlockSpec((rows, 2, chan, width), lambda i: (i, 0, 0, 0)),
+        ),
+        scratch_shapes=[
+            pltpu.VMEM((chan, stations2, width), jnp.bfloat16),
+            pltpu.VMEM((stations2, stations2), jnp.float32),
+            pltpu.VMEM((rows * 2 * chan, width), jnp.float32),
+        ],
+        compiler_params=pltpu.CompilerParams(
+            dimension_semantics=("arbitrary",), vmem_limit_bytes=40 * 1024 * 1024
+        ),
+        name="beamform",
+    )(lanes, w, sgroup, bgroup, cos_table, sin_table, taps)
+
+
+def lane_body(
+    samples, analysis_taps, synthesis_taps, antenna_station, station_group, beam_group, beam_weights
+):
+    n_row, n_col, n_sub = (lax.axis_size(name) for name in ("row", "col", "sub"))
+    local, _, chan, width = samples.shape
+    n = n_row * n_col * n_sub
+    stations = station_group.shape[0]
+    x = samples.transpose(2, 1, 0, 3).reshape(chan, 2 * local, width)
+    chan_rows, _, block, _ = beam_weights.shape
+    beams = block // n_row
+    w = (
+        beam_weights.reshape(chan_rows, 2, n_row, beams, stations)
+        .transpose(2, 3, 0, 1, 4)
+        .reshape(n_row, beams, chan_rows * 2 * stations)
+    )
+    station_row = jnp.broadcast_to(antenna_station.reshape(n, 1, local), (n, 2, local)).reshape(1, -1)
+    lanes, w_all = exchange(
+        x, w, (station_row, 2 * stations), analysis_taps, n_row, n_col, n_sub
+    )
+    index = lax.axis_index(("col", "sub", "row"))
+    bgroup = lax.dynamic_slice_in_dim(beam_group, index * beams, beams, 0)[:, None]
+    sgroup = jnp.tile(station_group[:, 0], 2 * chan)[None, :]
+    angle = 2.0 * np.pi / chan * (np.arange(chan)[:, None] * np.arange(chan)[None, :] % chan)
+    spread = lambda t: jnp.asarray(
+        np.repeat(t / math.sqrt(chan), 2 * stations, axis=1).astype(np.float32)
+    )
+    taps = jnp.broadcast_to(synthesis_taps[:, :, None], synthesis_taps.shape + (128,))
+    tile_rows = stations // (n_col * n_sub)
+    vis, series = beamform(
+        lanes, w_all, sgroup, bgroup, spread(np.cos(angle)), spread(np.sin(angle)), taps,
+        (chan_rows, 2, tile_rows, stations), 8,
+    )
+    return vis, series
+
+
 def solution(mesh):
+    shape = mesh.shape
+    fits = (
+        shape["row"] * shape["col"] * shape["sub"] == 16 and shape["col"] == 2 and shape["sub"] == 2
+    )
     return jax.shard_map(
-        body,
+        lane_body if fits else body,
         mesh=mesh,
         in_specs=(
             P(("grp", "row", "col", "sub"), None, None, None),

time: 158 us -> 59.5 us (0.38)
  waiting for transfers between devices: 66.2 us -> 0 us
  Pallas kernels: 0 us -> 50.2 us
  blocking collectives: 20.6 us -> 0 us
  other arithmetic: 18.1 us -> 0 us
  local copies, waits for them, and re-layouts: 23.5 us -> 8.19 us
  between operations: 14.4 us -> 0.71 us
  matrix products: 10.3 us -> 0 us
  starting transfers between devices: 4.66 us -> 0 us
    pallas_call x0 -> x2, Pallas kernels: none -> 50.2 us  [the longest x1 34.8 us: exchange(): pl.pallas_call(functools.partial(exchange_kernel, n_row, n_col, n_sub), o...]
    all_to_all x1 -> x0, waiting for transfers between devices: 47.3 us -> none  [body(): lax.all_to_all(beams, 'row', split_axis=0, concat_axis=2, tiled=True)]
    all_to_all x1 -> x0, blocking collectives: 20.6 us -> none  [body(): lax.all_to_all(spectra, 'row', split_axis=2, concat_axis=0, tiled=True)]
    all_gather x1 -> x0, waiting for transfers between devices: 18.9 us -> none  [body(): shard_rows = lax.all_gather(turned, ('col', 'sub'), axis=0, tiled=True)]
    add x1 -> x0, other arithmetic: 17.3 us -> none  [polyphase(): output = output + coefficients[tap_index][:, None] * shifted]
    dot_general x11 -> x0, matrix products: 10.3 us -> none  [the longest x1 5.12 us: body(): jnp.einsum('aqcf,qcpk->apkf', filtered, fourier_table(samples.shape[2], -...]
    all_to_all x4 -> x0, local copies, waits for them, and re-layouts: 7.02 us -> none  [the longest x3 6.19 us: body(): lax.all_to_all(beams, 'row', split_axis=0, concat_axis=2, tiled=True)]
    all_to_all x1 -> x0, starting transfers between devices: 4.62 us -> none  [body(): lax.all_to_all(beams, 'row', split_axis=0, concat_axis=2, tiled=True)]
  transfers between devices with their start and end apart: 2 -> 0, of which waited for: 2 -> 0; matrix products, arithmetic and copies ran while one was open for 3% -> 0% of each run, Pallas kernels for 0% -> 0%
where the time goes in v1:
time: 59.5 us; the launch traced here: 59.1 us
  Pallas kernels  50.2 us (84%)
  local copies, waits for them, and re-layouts  8.19 us (14%)
  between operations  0.71 us (1%)
    pallas_call x1, Pallas kernels, exchange(): pl.pallas_call(functools.partial(exchange_kernel, n_row, n_col, n_sub), o...  34.8 us
    pallas_call x1, Pallas kernels, beamform(): pl.pallas_call(beam_kernel, grid=(beams // rows,), out_shape=(jax.ShapeDt...  15.4 us
    unnamed x8, local copies, waits for them, and re-layouts  3.04 us
    transpose x1, local copies, waits for them, and re-layouts, lane_body(): x = samples.transpose(2, 1, 0, 3).reshape(chan, 2 * local, width)  1.34 us

profile of v1, /device:TPU:0, one launch (start us, length us, event | category | flops | bytes accessed | tf_op | source)
XLA Modules:
  0.0 59.1 jit_solution(14472262480987802414)
XLA Ops:
  0.6 0.0 copy-start
  0.7 0.7 %copy-done = s32[1024]{0:T(1024)S(1)} copy-done((s32[1024]{0:T(1024)S(1)}, s32[1024]{0:T(1024)}, u32[]{:S(2)}) %copy-start) | copy-done | bytes 4120
  1.3 0.1 dynamic-slice_bitcast_fusion
  1.4 0.8 %broadcast_in_dim.16 = s32[16,16]{1,0:T(8,128)S(1)} reshape(s32[256]{0:T(256)} %param.12) | data formatting | bytes 2048 | tf_op jit(solution)/shard_map/broadcast_in_dim | solution.py:458
  2.2 0.1 reshape.23.station_ref
  2.3 0.7 %tile.8 = s32[32,32]{1,0:T(8,128)S(1)} broadcast(s32[32]{0:T(128)} %bitcast.15), dimensions={1} | broadcast | bytes 4224 | tf_op jit(solution)/shard_map/tile | solution.py:464
  2.9 0.1 broadcast_in_dim_tile.3.sgroup_ref
  3.0 0.1 copy.17.bgroup_ref
  3.1 0.8 %broadcast_in_dim.19.taps_ref = f32[16,16,128]{2,1,0:T(8,128)S(1)} broadcast(f32[16,16]{1,0:T(8,128)} %param.11), dimensions={0,1} | broadcast | bytes 132096 | tf_op jit(solution)/shard_map/broadcast_in_dim | solution.py:469
  3.9 1.1 %reshape.21 = bf16[4,2,4,64,32]{3,2,4,1,0:T(4,128)(2,1)S(1)} reshape(bf16[4,2,256,32]{2,3,1,0:T(8,128)(2,1)} %param.15) | data formatting | bytes 262144 | tf_op jit(solution)/shard_map/reshape | solution.py:454
  5.0 0.1 copy.16.w_ref
  5.2 1.3 %copy.14 = bf16[16,2,16,512]{3,2,1,0:T(8,128)(2,1)S(1)} copy(bf16[16,2,16,512]{3,0,1,2:T(8,128)(2,1)} %bitcast.14) | data formatting | bytes 1048576 | tf_op jit(solution)/shard_map/transpose | solution.py:450
  6.5 0.0 copy-start.3
  6.5 0.7 %copy-done.3 = f32[16,16]{1,0:T(8,128)S(1)} copy-done((f32[16,16]{1,0:T(8,128)S(1)}, f32[16,16]{1,0:T(8,128)}, u32[]{:S(2)}) %copy-start.3) | copy-done | bytes 1048
  7.2 34.8 %exchange.1 = (bf16[16,64,512]{2,1,0:T(8,128)(2,1)S(1)}, bf16[4,64,256]{2,1,0:T(8,128)(2,1)S(1)}) custom-call(bf16[16,32,512]{2,1,0:T(8,128)(2,1)S(1)} %bitcast.12, bf16[4,64,256]{2,1,0:T(8,128)(2,1)S(1)} %copy.16.w_ref, s32[1,512]{1,0:T(1,128)S(1)} %reshape.23.station_ref, f32[16,16]{1,0:T(8,128)S(1)} %copy-done.3), custom_call_target="tpu_custom_call" | custom-call | tf_op jit(solution)/shard_map/exchange/pallas_call | solution.py:263
  42.0 0.0 copy-start.1
  42.0 0.8 %copy-done.1 = f32[16,1024]{1,0:T(8,128)S(1)} copy-done((f32[16,1024]{1,0:T(8,128)S(1)}, f32[16,1024]{1,0:T(8,128)}, u32[]{:S(2)}) %copy-start.1) | copy-done | bytes 65560
  42.8 0.0 copy-start.2
  42.9 0.8 %copy-done.2 = f32[16,1024]{1,0:T(8,128)S(1)} copy-done((f32[16,1024]{1,0:T(8,128)S(1)}, f32[16,1024]{1,0:T(8,128)}, u32[]{:S(2)}) %copy-start.2) | copy-done | bytes 65560
  43.7 15.4 %beamform.1 = (f32[4,2,8,32]{3,2,1,0:T(8,128)}, f32[64,2,16,512]{3,2,1,0:T(8,128)}) custom-call(bf16[16,64,512]{2,1,0:T(8,128)(2,1)S(1)} %get-tuple-element.4.lanes_ref, bf16[4,64,256]{2,1,0:T(8,128)(2,1)S(1)} %get-tuple-element.5.w_ref, s32[1,1024]{1,0:T(1,128)S(1)} %broadcast_in_dim_tile.3.sgroup_ref, s32[64,1]{1,0:T(8,128)S(1)} %copy.17.bgroup_ref, ...), custom_call_target="tpu_custom_call" | custom-call | tf_op jit(solution)/shard_map/beamform/pallas_call | solution.py:411
  (2 shorter events, 0.1 us)
Async XLA Ops:
  0.6 0.7 %copy-start = (s32[1024]{0:T(1024)S(1)}, s32[1024]{0:T(1024)}, u32[]{:S(2)}) copy-start(s32[1024]{0:T(1024)} %param.14) | copy-start | bytes 12292
  6.5 0.7 %copy-start.3 = (f32[16,16]{1,0:T(8,128)S(1)}, f32[16,16]{1,0:T(8,128)}, u32[]{:S(2)}) copy-start(f32[16,16]{1,0:T(8,128)} %taps_ref.1) | copy-start | bytes 3076
  42.0 0.8 %copy-start.1 = (f32[16,1024]{1,0:T(8,128)S(1)}, f32[16,1024]{1,0:T(8,128)}, u32[]{:S(2)}) copy-start(f32[16,1024]{1,0:T(8,128)} %constant.26.clone.sin_ref) | copy-start | bytes 196612
  42.8 0.8 %copy-start.2 = (f32[16,1024]{1,0:T(8,128)S(1)}, f32[16,1024]{1,0:T(8,128)}, u32[]{:S(2)}) copy-start(f32[16,1024]{1,0:T(8,128)} %constant.25.clone.cos_ref) | copy-start | bytes 196612

commit v2 on v0

--- a/solution.py
+++ b/solution.py
@@ -1,9 +1,14 @@
+import functools
 import math
 
 import jax
 import jax.numpy as jnp
 from jax import lax
+from jax.experimental import pallas as pl
+from jax.experimental.pallas import tpu as pltpu
 from jax.sharding import PartitionSpec as P
+
+MESH = pl.DeviceIdType.MESH
 
 ANTENNAS_PER_STN = 8
 SPEC = 512
@@ -111,9 +116,482 @@
     return (visibilities, beam_series)
 
 
+def exchange_kernel(
+    n_row, n_col, n_sub,
+    samples_hbm, w_hbm, station_hbm, taps_hbm, sgroup_hbm, bgroup_hbm,
+    lanes_ref, matrix_ref,
+    samples_ref, w_ref, station_ref, taps_ref, sgroup_ref, bgroup_ref,
+    x_ref, recv, w_mine, w_all, plain_ref, swapped_ref,
+    load_sem, own_sem, send_sem, recv_sem, w_send, w_recv, g_send, g_recv,
+):
+    n = n_row * n_col * n_sub
+    row, col, sub = lax.axis_index("row"), lax.axis_index("col"), lax.axis_index("sub")
+    me = (row * n_col + col) * n_sub + sub
+    halves, _, stations2, width = lanes_ref.shape
+    stations = stations2 // 2
+    local = samples_ref.shape[0]
+    chan = n
+    f32, bf16 = jnp.float32, jnp.bfloat16
+
+    def coords(index):
+        return {
+            "row": lax.div(index, n_col * n_sub),
+            "col": lax.rem(lax.div(index, n_sub), n_col),
+            "sub": lax.rem(index, n_sub),
+        }
+
+    barrier = pltpu.get_barrier_semaphore()
+
+    def greet(step, carry):
+        pl.semaphore_signal(
+            barrier, inc=1, device_id=coords(lax.rem(me + step, n)), device_id_type=MESH
+        )
+        return carry
+
+    lax.fori_loop(1, n, greet, 0)
+    pairs = [
+        (samples_hbm, samples_ref), (w_hbm, w_ref), (station_hbm, station_ref),
+        (taps_hbm, taps_ref), (sgroup_hbm, sgroup_ref), (bgroup_hbm, bgroup_ref),
+    ]
+    loads = [pltpu.make_async_copy(a, b, load_sem.at[i]) for i, (a, b) in enumerate(pairs)]
+    for load in loads:
+        load.start()
+
+    total = local * 2 * chan
+    block = 128
+    loads[0].wait()
+    source = samples_ref[...].reshape(total, halves * width)
+    for start in range(0, total, block):
+        to = lax.broadcasted_iota(jnp.int32, (block, total), 0) + start
+        origin = lax.broadcasted_iota(jnp.int32, (block, total), 1)
+        wanted = (
+            lax.rem(to, local) * (2 * chan)
+            + lax.rem(lax.div(to, local), 2) * chan
+            + lax.div(to, 2 * local)
+        )
+        turn = jnp.where(origin == wanted, 1.0, 0.0).astype(bf16)
+        turned = jnp.dot(turn, source, preferred_element_type=f32).astype(bf16)
+        lanes_here = block // (2 * local)
+        first = start // (2 * local)
+        for h in range(halves):
+            x_ref[first : first + lanes_here, h] = turned[:, h * width : (h + 1) * width].reshape(
+                lanes_here, 2, local, width
+            )
+    for load in loads[1:]:
+        load.wait()
+    beams = w_mine.shape[1]
+    flipped = w_ref[...].astype(f32).T.astype(bf16)
+    for r in range(n_row):
+        w_mine[r] = flipped[r * beams : (r + 1) * beams]
+    for h in range(halves):
+        recv[h, :, me] = x_ref[me, h]
+    w_all[row] = w_mine[row]
+
+    pl.semaphore_wait(barrier, n - 1)
+
+    def slab(h, step):
+        peer = lax.rem(me + step, n)
+        return pltpu.make_async_remote_copy(
+            src_ref=x_ref.at[peer, h], dst_ref=recv.at[h, :, me],
+            send_sem=send_sem.at[h, step], recv_sem=recv_sem.at[h, step],
+            device_id=coords(peer), device_id_type=MESH,
+        )
+
+    def weight(step):
+        peer = lax.rem(row + step, n_row)
+        return pltpu.make_async_remote_copy(
+            src_ref=w_mine.at[peer], dst_ref=w_all.at[row],
+            send_sem=w_send.at[step], recv_sem=w_recv.at[step],
+            device_id={"row": peer, "col": col, "sub": sub}, device_id_type=MESH,
+        )
+
+    for step in range(1, n_row):
+        weight(step).start()
+    for h in range(halves):
+
+        def start_slab(step, carry, h=h):
+            slab(h, step).start()
+            return carry
+
+        lax.fori_loop(1, n, start_slab, 0)
+
+    def column(values, offset, size):
+        there = lax.broadcasted_iota(jnp.int32, (size, values.shape[1]), 1)
+        here = lax.broadcasted_iota(jnp.int32, (size, values.shape[1]), 0) + offset
+        return jnp.sum(jnp.where(there == here, values, 0.0), axis=1, keepdims=True)
+
+    across = bgroup_ref.shape[1]
+    begin = ((col * n_sub + sub) * n_row + row) * beams
+    own_groups = column(
+        bgroup_ref[pl.ds(lax.div(begin, across), 1), :].astype(f32), lax.rem(begin, across), beams
+    )
+    groups = sgroup_ref[...].astype(f32)
+    members = jnp.where(groups == own_groups, 1.0, 0.0)
+    scaling = 1.0 / jnp.sqrt(jnp.sum(members, axis=1, keepdims=True))
+    mask = jnp.concatenate([members] * (128 // stations), axis=1)
+    mask = jnp.concatenate([mask] * (chan * stations2 // 128), axis=1)
+    for step in range(1, n_row):
+        weight(step).wait_recv()
+    columns = chan * stations2
+    weights = jnp.concatenate([w_all[r] for r in range(n_row)], axis=1).astype(f32)
+    weights = jnp.where(mask > 0.5, weights, 0.0) * scaling
+    position = lax.broadcasted_iota(jnp.int32, (beams, columns), 1)
+    first_half = lax.rem(position, stations2) < stations
+    plain_ref[...] = jnp.where(first_half, weights, -weights)
+    swapped_ref[...] = jnp.where(
+        first_half, pltpu.roll(weights, columns - stations, 1), pltpu.roll(weights, stations, 1)
+    )
+    turn_index = lax.rem(
+        lax.broadcasted_iota(jnp.int32, (chan, columns), 0)
+        * lax.div(lax.broadcasted_iota(jnp.int32, (chan, columns), 1), stations2),
+        chan,
+    )
+    cos_table = jnp.zeros((chan, columns), f32)
+    sin_table = jnp.zeros((chan, columns), f32)
+    for m in range(chan):
+        angle = 2 * math.pi * m / chan
+        hit = turn_index == m
+        cos_table = jnp.where(hit, math.cos(angle) / math.sqrt(chan), cos_table)
+        sin_table = jnp.where(hit, math.sin(angle) / math.sqrt(chan), sin_table)
+
+    def fill(index, carry):
+        low = pl.multiple_of(index * 8, 8)
+        plain, swapped = plain_ref[pl.ds(low, 8), :], swapped_ref[pl.ds(low, 8), :]
+        for b in range(8):
+            a0, a1 = plain[b : b + 1], swapped[b : b + 1]
+            at = pl.multiple_of((low + b) * 2 * chan, 2 * chan)
+            matrix_ref[pl.ds(at, chan), :] = (cos_table * a0 - sin_table * a1).astype(bf16)
+            matrix_ref[pl.ds(at + chan, chan), :] = (cos_table * a1 + sin_table * a0).astype(bf16)
+        return carry
+
+    lax.fori_loop(0, beams // 8, fill, 0)
+
+    place = lax.broadcasted_iota(jnp.int32, (stations, n * local), 0)
+    one_hot = jnp.where(place == station_ref[...], 1.0, 0.0).astype(bf16)
+    lane_index = lax.broadcasted_iota(jnp.int32, taps_ref.shape, 1)
+    own_taps = jnp.sum(jnp.where(lane_index == me, taps_ref[...], 0.0), axis=1, keepdims=True)
+    own_taps = own_taps * (1.0 / math.sqrt(ANTENNAS_PER_STN * n))
+    frame = lax.broadcasted_iota(jnp.int32, (stations2, 128), 1)
+
+    def forward(h, lane, slot, target):
+        return pltpu.make_async_remote_copy(
+            src_ref=lanes_ref.at[h, lane], dst_ref=lanes_ref.at[h, lane],
+            send_sem=g_send.at[slot], recv_sem=g_recv.at[h, lane],
+            device_id=target, device_id_type=MESH,
+        )
+
+    def lane_of(r, c, s):
+        return (r * n_col + c) * n_sub + s
+
+    other_col = {"row": row, "col": 1 - col, "sub": sub}
+    other_sub = {"row": row, "col": col, "sub": 1 - sub}
+    sends = []
+
+    def send(h, lane, target):
+        copy = forward(h, lane, len(sends), target)
+        copy.start()
+        sends.append(copy)
+
+    def arrived(h, lane):
+        forward(h, lane, 0, other_sub).wait_recv()
+
+    def filter_half(h, last):
+        def finish_slab(step, carry):
+            slab(h, step).wait_recv()
+            return carry
+
+        lax.fori_loop(1, n, finish_slab, 0)
+        summed = jnp.concatenate(
+            [
+                jnp.dot(
+                    one_hot, recv[h, q].reshape(n * local, width), preferred_element_type=f32
+                )
+                for q in range(2)
+            ],
+            axis=0,
+        )
+        for start in range(0, width, 128):
+            tile = summed[:, start : start + 128]
+            result = own_taps[0:1] * tile
+            for tap in range(1, taps_ref.shape[0]):
+                moved = jnp.where(
+                    frame >= tap, pltpu.roll(tile, tap, 1), pltpu.roll(last, tap, 1)
+                )
+                result = result + own_taps[tap : tap + 1] * moved
+            lanes_ref[h, me, :, start : start + 128] = result.astype(bf16)
+            last = tile
+        return last
+
+    def spread_own(h):
+        for step in range(1, n_row):
+            send(h, me, {"row": lax.rem(row + step, n_row), "col": col, "sub": sub})
+        send(h, me, other_col)
+        send(h, me, other_sub)
+
+    def spread_row(h):
+        for step in range(1, n_row):
+            lane = lane_of(lax.rem(row + n_row - step, n_row), col, sub)
+            arrived(h, lane)
+            send(h, lane, other_col)
+            send(h, lane, other_sub)
+
+    def spread_col(h):
+        for step in range(n_row):
+            lane = lane_of(lax.rem(row + n_row - step, n_row), 1 - col, sub)
+            arrived(h, lane)
+            send(h, lane, other_sub)
+
+    last = jnp.zeros((stations2, 128), f32)
+    for h in range(halves):
+        last = filter_half(h, last)
+        spread_own(h)
+        if h > 0:
+            spread_col(h - 1)
+        spread_row(h)
+    spread_col(halves - 1)
+    for h in range(halves):
+        for step in range(n_row):
+            for c in range(n_col):
+                arrived(h, lane_of(lax.rem(row + n_row - step, n_row), c, 1 - sub))
+    for copy in sends:
+        copy.wait_send()
+    for h in range(halves):
+
+        def finish_send(step, carry, h=h):
+            slab(h, step).wait_send()
+            return carry
+
+        lax.fori_loop(1, n, finish_send, 0)
+    for step in range(1, n_row):
+        weight(step).wait_send()
+
+
+def exchange(samples, w, station, taps, sgroup, bgroup, n_row, n_col, n_sub, halves):
+    n = n_row * n_col * n_sub
+    local, _, chan, frames = samples.shape
+    stations = sgroup.shape[1]
+    stations2 = 2 * stations
+    width = frames // halves
+    kqs, block = w.shape
+    beams = block // n_row
+    any_space = pl.BlockSpec(memory_space=pl.ANY)
+    vmem = pl.BlockSpec(memory_space=pltpu.VMEM)
+    dma = pltpu.SemaphoreType.DMA
+    sends = ((n_row - 1) * 3 + 2 + n_row) * halves
+    bf16 = jnp.bfloat16
+    inputs = (samples, w, station, taps, sgroup, bgroup)
+    return pl.pallas_call(
+        functools.partial(exchange_kernel, n_row, n_col, n_sub),
+        out_shape=(
+            jax.ShapeDtypeStruct((halves, n, stations2, width), bf16),
+            jax.ShapeDtypeStruct((beams * 2 * chan, chan * stations2), bf16),
+        ),
+        in_specs=[any_space] * 6,
+        out_specs=(vmem, vmem),
+        scratch_shapes=[pltpu.VMEM(a.shape, a.dtype) for a in inputs]
+        + [
+            pltpu.VMEM((chan, halves, 2, local, width), bf16),
+            pltpu.VMEM((halves, 2, n, local, width), bf16),
+            pltpu.VMEM((n_row, beams, kqs), bf16),
+            pltpu.VMEM((n_row, beams, kqs), bf16),
+            pltpu.VMEM((beams, chan * stations2), jnp.float32),
+            pltpu.VMEM((beams, chan * stations2), jnp.float32),
+            dma((len(inputs),)), dma((2,)), dma((halves, n)), dma((halves, n)),
+            dma((n_row,)), dma((n_row,)), dma((sends,)), dma((halves, n)),
+        ],
+        compiler_params=pltpu.CompilerParams(
+            collective_id=0, has_side_effects=True, vmem_limit_bytes=24 * 1024 * 1024
+        ),
+        name="exchange",
+    )(*inputs)
+
+
+def fourier(points):
+    count = len(points)
+    if count == 1:
+        return points
+    even, odd = fourier(points[0::2]), fourier(points[1::2])
+    half = count // 2
+    low, high = [], []
+    for index in range(half):
+        (er, ei), (r, i) = even[index], odd[index]
+        if index == 0:
+            tr, ti = r, i
+        elif 4 * index == count:
+            tr, ti = i, -r
+        else:
+            c, s = math.cos(2 * math.pi * index / count), math.sin(2 * math.pi * index / count)
+            if 8 * index == count:
+                tr, ti = (r + i) * c, (i - r) * c
+            elif 8 * index == 3 * count:
+                tr, ti = (i - r) * s, -(r + i) * s
+            else:
+                tr, ti = r * c + i * s, i * c - r * s
+        low.append((er + tr, ei + ti))
+        high.append((er - tr, ei - ti))
+    return low + high
+
+def beam_kernel(
+    lanes_ref, matrix_ref, taps_ref, vis_ref, out_ref,
+    spectra, gram, even_ref, odd_ref, wide_taps,
+):
+    halves, chan, stations2, width = lanes_ref.shape
+    stations = stations2 // 2
+    frames = halves * width
+    step_index = pl.program_id(0)
+    rows = out_ref.shape[0] // 2
+    size = rows * 2 * chan
+    count = matrix_ref.shape[0] // size
+
+    def product(index):
+        at = pl.multiple_of(index * size, size)
+        return jnp.dot(
+            matrix_ref[pl.ds(at, size), :],
+            spectra[...].reshape(chan * stations2, frames),
+            preferred_element_type=jnp.float32,
+        )
+
+    @pl.when(step_index == 0)
+    def _():
+        step_rows = 16
+
+        @pl.loop(0, stations // step_rows)
+        def _(block):
+            low = pl.multiple_of(block * step_rows, step_rows)
+            for start in range(0, frames, 128):
+                h, inner = divmod(start, width)
+                points = [
+                    tuple(
+                        lanes_ref[
+                            h, c, pl.ds(low + q * stations, step_rows), inner : inner + 128
+                        ].astype(jnp.float32)
+                        for q in range(2)
+                    )
+                    for c in range(chan)
+                ]
+                for k, parts in enumerate(fourier(points)):
+                    for q, value in enumerate(parts):
+                        spectra[
+                            k, pl.ds(low + q * stations, step_rows), start : start + 128
+                        ] = value.astype(jnp.bfloat16)
+
+        chan_rows, _, own, _ = vis_ref.shape
+        first = lax.axis_index("row") * chan_rows
+        block_index = lax.axis_index(("col", "sub"))
+        begin = pl.multiple_of(block_index * own, own)
+        for k in range(chan_rows):
+            block = spectra[first + k]
+            gram[k] = lax.dot_general(
+                block, block, (((1,), (1,)), ((), ())), preferred_element_type=jnp.float32
+            )
+            top = gram[k, pl.ds(begin, own), :]
+            bottom = gram[k, pl.ds(begin + stations, own), :]
+            vis_ref[k, 0] = (top[:, :stations] + bottom[:, stations:]) * (1.0 / frames)
+            vis_ref[k, 1] = (bottom[:, :stations] - top[:, stations:]) * (1.0 / frames)
+
+        for tap in range(taps_ref.shape[0]):
+            there = lax.broadcasted_iota(jnp.int32, (chan, chan), 1)
+            here = lax.broadcasted_iota(jnp.int32, (chan, chan), 0)
+            values = jnp.where(there == here, taps_ref[tap : tap + 1, :], 0.0)
+            wide_taps[tap] = jnp.broadcast_to(
+                jnp.sum(values, axis=1, keepdims=True), (chan, 128)
+            )
+        even_ref[...] = product(0)
+
+    lane = lax.broadcasted_iota(jnp.int32, (chan, 128), 1)
+
+    def shift(tiles, amount):
+        turned = [pltpu.roll(tile, amount, 1) for tile in tiles]
+        before = [jnp.zeros_like(turned[0])] + turned[:-1]
+        return [jnp.where(lane >= amount, t, b) for t, b in zip(turned, before)]
+
+    taps = taps_ref.shape[0]
+    stride = 4
+
+    def synthesize(inverse, offset):
+        for index in range(2 * rows):
+            tiles = [
+                inverse[index * chan : (index + 1) * chan, start : start + 128]
+                for start in range(0, frames, 128)
+            ]
+            moved = [tiles]
+            for amount in range(1, stride):
+                moved.append(shift(tiles, amount))
+            total_tiles = None
+            for high in range(taps // stride - 1, -1, -1):
+                if total_tiles is not None:
+                    total_tiles = shift(total_tiles, stride)
+                for low in range(stride):
+                    tap = wide_taps[high * stride + low]
+                    terms = [tap * tile for tile in moved[low]]
+                    total_tiles = (
+                        terms
+                        if total_tiles is None
+                        else [a + t for a, t in zip(total_tiles, terms)]
+                    )
+            for number, tile in enumerate(total_tiles):
+                out_ref[offset + index // 2, index % 2, :, number * 128 : (number + 1) * 128] = tile
+
+    odd_ref[...] = product(2 * step_index + 1)
+    synthesize(even_ref, 0)
+    even_ref[...] = product(jnp.minimum(2 * step_index + 2, count - 1))
+    synthesize(odd_ref, rows)
+
+
+def beamform(lanes, matrix, taps, vis_shape, rows):
+    halves, chan, stations2, width = lanes.shape
+    frames = halves * width
+    beams = matrix.shape[0] // (2 * chan)
+    whole = lambda *shape: pl.BlockSpec(shape, lambda i: (0,) * len(shape))
+    vmem = pl.BlockSpec(memory_space=pltpu.VMEM)
+    return pl.pallas_call(
+        beam_kernel,
+        grid=(beams // (2 * rows),),
+        out_shape=(
+            jax.ShapeDtypeStruct(vis_shape, jnp.float32),
+            jax.ShapeDtypeStruct((beams, 2, chan, frames), jnp.float32),
+        ),
+        in_specs=[vmem, vmem, vmem],
+        out_specs=(
+            whole(*vis_shape),
+            pl.BlockSpec((2 * rows, 2, chan, frames), lambda i: (i, 0, 0, 0)),
+        ),
+        scratch_shapes=[
+            pltpu.VMEM((chan, stations2, frames), jnp.bfloat16),
+            pltpu.VMEM((vis_shape[0], stations2, stations2), jnp.float32),
+            pltpu.VMEM((rows * 2 * chan, frames), jnp.float32),
+            pltpu.VMEM((rows * 2 * chan, frames), jnp.float32),
+            pltpu.VMEM((taps.shape[0], chan, 128), jnp.float32),
+        ],
+        compiler_params=pltpu.CompilerParams(
+            dimension_semantics=("arbitrary",), vmem_limit_bytes=24 * 1024 * 1024
+        ),
+        name="beamform",
+    )(lanes, matrix, taps)
+
+
+def lane_body(
+    samples, analysis_taps, synthesis_taps, antenna_station, station_group, beam_group, beam_weights
+):
+    n_row, n_col, n_sub = (lax.axis_size(name) for name in ("row", "col", "sub"))
+    stations = station_group.shape[0]
+    chan_rows, _, block, _ = beam_weights.shape
+    w = beam_weights.transpose(0, 1, 3, 2).reshape(chan_rows * 2 * stations, block)
+    lanes, matrix = exchange(
+        samples, w, antenna_station.reshape(1, -1), analysis_taps,
+        station_group.reshape(1, -1), beam_group.reshape(-1, 128), n_row, n_col, n_sub, 2,
+    )
+    tile_rows = stations // (n_col * n_sub)
+    return beamform(lanes, matrix, synthesis_taps, (chan_rows, 2, tile_rows, stations), 8)
+
+
 def solution(mesh):
+    shape = mesh.shape
+    fits = (
+        shape["row"] * shape["col"] * shape["sub"] == 16 and shape["col"] == 2 and shape["sub"] == 2
+    )
     return jax.shard_map(
-        body,
+        lane_body if fits else body,
         mesh=mesh,
         in_specs=(
             P(("grp", "row", "col", "sub"), None, None, None),

time: 158 us -> 71.1 us (0.45)
  waiting for transfers between devices: 66.2 us -> 0 us
  Pallas kernels: 0 us -> 64.8 us
  blocking collectives: 20.6 us -> 0 us
  local copies, waits for them, and re-layouts: 23.5 us -> 5.35 us
  other arithmetic: 18.1 us -> 0 us
  between operations: 14.4 us -> 0.66 us
  matrix products: 10.3 us -> 0 us
  starting transfers between devices: 4.66 us -> 0 us
    pallas_call x0 -> x2, Pallas kernels: none -> 64.8 us  [the longest x1 34.9 us: exchange(): pl.pallas_call(functools.partial(exchange_kernel, n_row, n_col, n_sub), o...]
    all_to_all x1 -> x0, waiting for transfers between devices: 47.3 us -> none  [body(): lax.all_to_all(beams, 'row', split_axis=0, concat_axis=2, tiled=True)]
    all_to_all x1 -> x0, blocking collectives: 20.6 us -> none  [body(): lax.all_to_all(spectra, 'row', split_axis=2, concat_axis=0, tiled=True)]
    all_gather x1 -> x0, waiting for transfers between devices: 18.9 us -> none  [body(): shard_rows = lax.all_gather(turned, ('col', 'sub'), axis=0, tiled=True)]
    add x1 -> x0, other arithmetic: 17.3 us -> none  [polyphase(): output = output + coefficients[tap_index][:, None] * shifted]
    dot_general x11 -> x0, matrix products: 10.3 us -> none  [the longest x1 5.12 us: body(): jnp.einsum('aqcf,qcpk->apkf', filtered, fourier_table(samples.shape[2], -...]
    all_to_all x4 -> x0, local copies, waits for them, and re-layouts: 7.02 us -> none  [the longest x3 6.19 us: body(): lax.all_to_all(beams, 'row', split_axis=0, concat_axis=2, tiled=True)]
    all_to_all x1 -> x0, starting transfers between devices: 4.62 us -> none  [body(): lax.all_to_all(beams, 'row', split_axis=0, concat_axis=2, tiled=True)]
  transfers between devices with their start and end apart: 2 -> 0, of which waited for: 2 -> 0; matrix products, arithmetic and copies ran while one was open for 3% -> 0% of each run, Pallas kernels for 0% -> 0%
where the time goes in v2:
time: 71.1 us; the launch traced here: 70.8 us
  Pallas kernels  64.8 us (91%)
  local copies, waits for them, and re-layouts  5.35 us (8%)
    pallas_call x1, Pallas kernels, exchange(): pl.pallas_call(functools.partial(exchange_kernel, n_row, n_col, n_sub), o...  34.9 us
    pallas_call x1, Pallas kernels, beamform(): pl.pallas_call(beam_kernel, grid=(beams // (2 * rows),), out_shape=(jax.S...  29.8 us
    unnamed x14, local copies, waits for them, and re-layouts  5.35 us

profile of v2, /device:TPU:0, one launch (start us, length us, event | category | flops | bytes accessed | tf_op | source)
XLA Modules:
  0.0 70.8 jit_solution(17505802474356472426)
XLA Ops:
  0.6 0.0 copy-start
  0.6 1.0 %copy-done = bf16[16,2,16,512]{3,2,1,0:T(8,128)(2,1)S(1)} copy-done((bf16[16,2,16,512]{3,2,1,0:T(8,128)(2,1)S(1)}, bf16[16,2,16,512]{3,2,1,0:T(8,128)(2,1)}, u32[]{:S(2)}) %copy-start) | copy-done | bytes 524312
  1.7 0.0 copy-start.1
  1.7 0.9 %copy-done.1 = bf16[4,2,256,32]{2,3,1,0:T(8,128)(2,1)S(1)} copy-done((bf16[4,2,256,32]{2,3,1,0:T(8,128)(2,1)S(1)}, bf16[4,2,256,32]{2,3,1,0:T(8,128)(2,1)}, u32[]{:S(2)}) %copy-start.1) | copy-done | bytes 131096
  2.6 0.0 copy-start.2
  2.6 0.7 copy-done.2
  3.3 0.0 copy-start.4
  3.3 0.7 copy-done.4
  4.0 0.0 copy-start.5
  4.0 0.7 copy-done.5
  4.6 0.0 copy-start.6
  4.6 0.7 copy-done.6
  5.3 34.9 %exchange.1 = (bf16[2,16,64,256]{3,2,1,0:T(8,128)(2,1)S(1)}, bf16[2048,1024]{1,0:T(8,128)(2,1)S(1)}) custom-call(bf16[16,2,16,512]{3,2,1,0:T(8,128)(2,1)S(1)} %copy-done, bf16[256,256]{1,0:T(8,128)(2,1)S(1)} %bitcast.6, s32[1,256]{1,0:T(1,128)S(1)} %bitcast.8, f32[16,16]{1,0:T(8,128)S(1)} %copy-done.2, s32[1,32]{1,0:T(1,128)S(1)} %bitcast.9, ...), custom_call_target="tpu_custom_call" | custom-call | tf_op jit(solution)/shard_map/exchange/pallas_call | solution.py:383
  40.2 0.0 copy-start.3
  40.2 0.7 copy-done.3
  40.9 29.8 %beamform.1 = (f32[4,2,8,32]{3,2,1,0:T(8,128)}, f32[64,2,16,512]{3,2,1,0:T(8,128)}) custom-call(bf16[2,16,64,256]{3,2,1,0:T(8,128)(2,1)S(1)} %get-tuple-element.4.lanes_ref, bf16[2048,1024]{1,0:T(8,128)(2,1)S(1)} %get-tuple-element.5.matrix_ref, f32[16,16]{1,0:T(8,128)S(1)} %copy-done.3), custom_call_target="tpu_custom_call" | custom-call | tf_op jit(solution)/shard_map/beamform/pallas_call | solution.py:547
Async XLA Ops:
  0.6 1.0 %copy-start = (bf16[16,2,16,512]{3,2,1,0:T(8,128)(2,1)S(1)}, bf16[16,2,16,512]{3,2,1,0:T(8,128)(2,1)}, u32[]{:S(2)}) copy-start(bf16[16,2,16,512]{3,2,1,0:T(8,128)(2,1)} %samples_hbm.1) | copy-start | bytes 1572868
  1.7 0.9 %copy-start.1 = (bf16[4,2,256,32]{2,3,1,0:T(8,128)(2,1)S(1)}, bf16[4,2,256,32]{2,3,1,0:T(8,128)(2,1)}, u32[]{:S(2)}) copy-start(bf16[4,2,256,32]{2,3,1,0:T(8,128)(2,1)} %param.13) | copy-start | bytes 393220
  2.6 0.7 copy-start.2
  3.3 0.7 copy-start.4
  4.0 0.7 copy-start.5
  4.6 0.7 copy-start.6
  40.2 0.7 copy-start.3

commit v3 on v2

--- a/solution.py
+++ b/solution.py
@@ -374,7 +374,7 @@
     width = frames // halves
     kqs, block = w.shape
     beams = block // n_row
-    any_space = pl.BlockSpec(memory_space=pl.ANY)
+    any_space = pl.BlockSpec(memory_space=pltpu.HBM)
     vmem = pl.BlockSpec(memory_space=pltpu.VMEM)
     dma = pltpu.SemaphoreType.DMA
     sends = ((n_row - 1) * 3 + 2 + n_row) * halves
@@ -433,15 +433,13 @@
 
 def beam_kernel(
     lanes_ref, matrix_ref, taps_ref, vis_ref, out_ref,
-    spectra, gram, even_ref, odd_ref, wide_taps,
+    spectra, gram, inverse_ref, wide_taps,
 ):
     halves, chan, stations2, width = lanes_ref.shape
     stations = stations2 // 2
     frames = halves * width
     step_index = pl.program_id(0)
-    rows = out_ref.shape[0] // 2
-    size = rows * 2 * chan
-    count = matrix_ref.shape[0] // size
+    size = out_ref.shape[0]
 
     def product(index):
         at = pl.multiple_of(index * size, size)
@@ -496,46 +494,44 @@
             wide_taps[tap] = jnp.broadcast_to(
                 jnp.sum(values, axis=1, keepdims=True), (chan, 128)
             )
-        even_ref[...] = product(0)
-
-    lane = lax.broadcasted_iota(jnp.int32, (chan, 128), 1)
+
+    lane = lax.broadcasted_iota(jnp.int32, (8, 128), 1)
+    later = [None] + [lane >= amount for amount in range(1, taps_ref.shape[0])]
 
     def shift(tiles, amount):
         turned = [pltpu.roll(tile, amount, 1) for tile in tiles]
         before = [jnp.zeros_like(turned[0])] + turned[:-1]
-        return [jnp.where(lane >= amount, t, b) for t, b in zip(turned, before)]
+        return [jnp.where(later[amount], t, b) for t, b in zip(turned, before)]
 
     taps = taps_ref.shape[0]
     stride = 4
-
-    def synthesize(inverse, offset):
-        for index in range(2 * rows):
-            tiles = [
-                inverse[index * chan : (index + 1) * chan, start : start + 128]
-                for start in range(0, frames, 128)
-            ]
-            moved = [tiles]
-            for amount in range(1, stride):
-                moved.append(shift(tiles, amount))
+    starts = range(0, frames, 128)
+
+    inverse_ref[...] = product(step_index)
+    for top in range(0, chan, 8):
+        tap_tiles = [wide_taps[tap, top : top + 8, :] for tap in range(taps)]
+
+        def one(index, carry, top=top, tap_tiles=tap_tiles):
+            at = pl.multiple_of(index * chan + top, 8)
+            tiles = [inverse_ref[pl.ds(at, 8), start : start + 128] for start in starts]
+            moved = [tiles] + [shift(tiles, amount) for amount in range(1, stride)]
             total_tiles = None
             for high in range(taps // stride - 1, -1, -1):
                 if total_tiles is not None:
                     total_tiles = shift(total_tiles, stride)
                 for low in range(stride):
-                    tap = wide_taps[high * stride + low]
+                    tap = tap_tiles[high * stride + low]
                     terms = [tap * tile for tile in moved[low]]
                     total_tiles = (
                         terms
                         if total_tiles is None
                         else [a + t for a, t in zip(total_tiles, terms)]
                     )
-            for number, tile in enumerate(total_tiles):
-                out_ref[offset + index // 2, index % 2, :, number * 128 : (number + 1) * 128] = tile
-
-    odd_ref[...] = product(2 * step_index + 1)
-    synthesize(even_ref, 0)
-    even_ref[...] = product(jnp.minimum(2 * step_index + 2, count - 1))
-    synthesize(odd_ref, rows)
+            for start, tile in zip(starts, total_tiles):
+                out_ref[pl.ds(at, 8), start : start + 128] = tile
+            return carry
+
+        lax.fori_loop(0, size // chan, one, 0, unroll=16)
 
 
 def beamform(lanes, matrix, taps, vis_shape, rows):
@@ -544,22 +540,21 @@
     beams = matrix.shape[0] // (2 * chan)
     whole = lambda *shape: pl.BlockSpec(shape, lambda i: (0,) * len(shape))
     vmem = pl.BlockSpec(memory_space=pltpu.VMEM)
-    return pl.pallas_call(
+    vis, series = pl.pallas_call(
         beam_kernel,
-        grid=(beams // (2 * rows),),
+        grid=(beams // rows,),
         out_shape=(
             jax.ShapeDtypeStruct(vis_shape, jnp.float32),
-            jax.ShapeDtypeStruct((beams, 2, chan, frames), jnp.float32),
+            jax.ShapeDtypeStruct((matrix.shape[0], frames), jnp.float32),
         ),
         in_specs=[vmem, vmem, vmem],
         out_specs=(
             whole(*vis_shape),
-            pl.BlockSpec((2 * rows, 2, chan, frames), lambda i: (i, 0, 0, 0)),
+            pl.BlockSpec((rows * 2 * chan, frames), lambda i: (i, 0)),
         ),
         scratch_shapes=[
             pltpu.VMEM((chan, stations2, frames), jnp.bfloat16),
             pltpu.VMEM((vis_shape[0], stations2, stations2), jnp.float32),
-            pltpu.VMEM((rows * 2 * chan, frames), jnp.float32),
             pltpu.VMEM((rows * 2 * chan, frames), jnp.float32),
             pltpu.VMEM((taps.shape[0], chan, 128), jnp.float32),
         ],
@@ -568,6 +563,7 @@
         ),
         name="beamform",
     )(lanes, matrix, taps)
+    return vis, series.reshape(beams, 2, chan, frames)
 
 
 def lane_body(

time: 71.1 us -> 56.4 us (0.79)
  Pallas kernels: 64.8 us -> 50.1 us
    pallas_call x1, Pallas kernels: 29.8 us -> 15.2 us  [beamform(): pl.pallas_call(beam_kernel, grid=(beams // rows,), out_shape=(jax.ShapeDt...]
where the time goes in v3:
time: 56.4 us; the launch traced here: 56.1 us
  Pallas kernels  50.1 us (89%)
  local copies, waits for them, and re-layouts  5.35 us (9%)
  between operations  0.66 us (1%)
    pallas_call x1, Pallas kernels, exchange(): pl.pallas_call(functools.partial(exchange_kernel, n_row, n_col, n_sub), o...  34.9 us
    pallas_call x1, Pallas kernels, beamform(): pl.pallas_call(beam_kernel, grid=(beams // rows,), out_shape=(jax.ShapeDt...  15.2 us
    unnamed x14, local copies, waits for them, and re-layouts  5.35 us

profile of v3, /device:TPU:0, one launch (start us, length us, event | category | flops | bytes accessed | tf_op | source)
XLA Modules:
  0.0 56.1 jit_solution(15570159286956414005)
XLA Ops:
  0.6 0.0 copy-start
  0.6 1.0 %copy-done = bf16[16,2,16,512]{3,2,1,0:T(8,128)(2,1)S(1)} copy-done((bf16[16,2,16,512]{3,2,1,0:T(8,128)(2,1)S(1)}, bf16[16,2,16,512]{3,2,1,0:T(8,128)(2,1)}, u32[]{:S(2)}) %copy-start) | copy-done | bytes 524312
  1.7 0.0 copy-start.1
  1.7 0.9 %copy-done.1 = bf16[4,2,256,32]{2,3,1,0:T(8,128)(2,1)S(1)} copy-done((bf16[4,2,256,32]{2,3,1,0:T(8,128)(2,1)S(1)}, bf16[4,2,256,32]{2,3,1,0:T(8,128)(2,1)}, u32[]{:S(2)}) %copy-start.1) | copy-done | bytes 131096
  2.6 0.0 copy-start.2
  2.6 0.7 %copy-done.2 = f32[16,16]{1,0:T(8,128)S(1)} copy-done((f32[16,16]{1,0:T(8,128)S(1)}, f32[16,16]{1,0:T(8,128)}, u32[]{:S(2)}) %copy-start.2) | copy-done | bytes 1048
  3.3 0.0 copy-start.4
  3.3 0.7 %copy-done.4 = s32[1024]{0:T(1024)S(1)} copy-done((s32[1024]{0:T(1024)S(1)}, s32[1024]{0:T(1024)}, u32[]{:S(2)}) %copy-start.4) | copy-done | bytes 4120
  4.0 0.0 copy-start.5
  4.0 0.7 %copy-done.5 = s32[256]{0:T(256)S(1)} copy-done((s32[256]{0:T(256)S(1)}, s32[256]{0:T(256)}, u32[]{:S(2)}) %copy-start.5) | copy-done | bytes 1048
  4.6 0.0 copy-start.6
  4.6 0.7 %copy-done.6 = s32[32,1]{0,1:T(1,128)S(1)} copy-done((s32[32,1]{0,1:T(1,128)S(1)}, s32[32,1]{0,1:T(1,128)}, u32[]{:S(2)}) %copy-start.6) | copy-done | bytes 152
  5.3 34.9 %exchange.1 = (bf16[2,16,64,256]{3,2,1,0:T(8,128)(2,1)S(1)}, bf16[2048,1024]{1,0:T(8,128)(2,1)S(1)}) custom-call(bf16[16,2,16,512]{3,2,1,0:T(8,128)(2,1)S(1)} %copy-done, bf16[256,256]{1,0:T(8,128)(2,1)S(1)} %bitcast.7, s32[1,256]{1,0:T(1,128)S(1)} %bitcast.9, f32[16,16]{1,0:T(8,128)S(1)} %copy-done.2, s32[1,32]{1,0:T(1,128)S(1)} %bitcast.10, ...), custom_call_target="tpu_custom_call" | custom-call | tf_op jit(solution)/shard_map/exchange/pallas_call | solution.py:383
  40.2 0.0 copy-start.3
  40.2 0.7 %copy-done.3 = f32[16,16]{1,0:T(8,128)S(1)} copy-done((f32[16,16]{1,0:T(8,128)S(1)}, f32[16,16]{1,0:T(8,128)}, u32[]{:S(2)}) %copy-start.3) | copy-done | bytes 1048
  40.9 15.2 %beamform.1 = (f32[4,2,8,32]{3,2,1,0:T(8,128)}, f32[2048,512]{1,0:T(8,128)}) custom-call(bf16[2,16,64,256]{3,2,1,0:T(8,128)(2,1)S(1)} %get-tuple-element.6.lanes_ref, bf16[2048,1024]{1,0:T(8,128)(2,1)S(1)} %get-tuple-element.7.matrix_ref, f32[16,16]{1,0:T(8,128)S(1)} %copy-done.3), custom_call_target="tpu_custom_call" | custom-call | tf_op jit(solution)/shard_map/beamform/pallas_call | solution.py:543
Async XLA Ops:
  0.6 1.0 %copy-start = (bf16[16,2,16,512]{3,2,1,0:T(8,128)(2,1)S(1)}, bf16[16,2,16,512]{3,2,1,0:T(8,128)(2,1)}, u32[]{:S(2)}) copy-start(bf16[16,2,16,512]{3,2,1,0:T(8,128)(2,1)} %samples_hbm.1) | copy-start | bytes 1572868
  1.7 0.9 %copy-start.1 = (bf16[4,2,256,32]{2,3,1,0:T(8,128)(2,1)S(1)}, bf16[4,2,256,32]{2,3,1,0:T(8,128)(2,1)}, u32[]{:S(2)}) copy-start(bf16[4,2,256,32]{2,3,1,0:T(8,128)(2,1)} %param.13) | copy-start | bytes 393220
  2.6 0.7 %copy-start.2 = (f32[16,16]{1,0:T(8,128)S(1)}, f32[16,16]{1,0:T(8,128)}, u32[]{:S(2)}) copy-start(f32[16,16]{1,0:T(8,128)} %taps_hbm.1) | copy-start | bytes 3076
  3.3 0.7 %copy-start.4 = (s32[1024]{0:T(1024)S(1)}, s32[1024]{0:T(1024)}, u32[]{:S(2)}) copy-start(s32[1024]{0:T(1024)} %param.12) | copy-start | bytes 12292
  4.0 0.7 %copy-start.5 = (s32[256]{0:T(256)S(1)}, s32[256]{0:T(256)}, u32[]{:S(2)}) copy-start(s32[256]{0:T(256)} %param.10) | copy-start | bytes 3076
  4.6 0.7 %copy-start.6 = (s32[32,1]{0,1:T(1,128)S(1)}, s32[32,1]{0,1:T(1,128)}, u32[]{:S(2)}) copy-start(s32[32,1]{0,1:T(1,128)} %param.11) | copy-start | bytes 388
  40.2 0.7 %copy-start.3 = (f32[16,16]{1,0:T(8,128)S(1)}, f32[16,16]{1,0:T(8,128)}, u32[]{:S(2)}) copy-start(f32[16,16]{1,0:T(8,128)} %taps_ref.1) | copy-start | bytes 3076

commit v4 on v3

--- a/solution.py
+++ b/solution.py
@@ -119,8 +119,8 @@
 def exchange_kernel(
     n_row, n_col, n_sub,
     samples_hbm, w_hbm, station_hbm, taps_hbm, sgroup_hbm, bgroup_hbm,
-    lanes_ref, matrix_ref,
-    samples_ref, w_ref, station_ref, taps_ref, sgroup_ref, bgroup_ref,
+    lanes_ref, matrix_hbm,
+    matrix_ref, samples_ref, w_ref, station_ref, taps_ref, sgroup_ref, bgroup_ref,
     x_ref, recv, w_mine, w_all, plain_ref, swapped_ref,
     load_sem, own_sem, send_sem, recv_sem, w_send, w_recv, g_send, g_recv,
 ):
@@ -207,13 +207,22 @@
 
     for step in range(1, n_row):
         weight(step).start()
-    for h in range(halves):
-
-        def start_slab(step, carry, h=h):
+
+    def start_half(h):
+        def start_slab(step, carry):
             slab(h, step).start()
             return carry
 
         lax.fori_loop(1, n, start_slab, 0)
+
+    def finish_half(h):
+        def finish_send(step, carry):
+            slab(h, step).wait_send()
+            return carry
+
+        lax.fori_loop(1, n, finish_send, 0)
+
+    start_half(0)
 
     def column(values, offset, size):
         there = lax.broadcasted_iota(jnp.int32, (size, values.shape[1]), 1)
@@ -265,6 +274,8 @@
         return carry
 
     lax.fori_loop(0, beams // 8, fill, 0)
+    matrix_copy = pltpu.make_async_copy(matrix_ref, matrix_hbm, own_sem.at[0])
+    matrix_copy.start()
 
     place = lax.broadcasted_iota(jnp.int32, (stations, n * local), 0)
     one_hot = jnp.where(place == station_ref[...], 1.0, 0.0).astype(bf16)
@@ -343,6 +354,9 @@
 
     last = jnp.zeros((stations2, 128), f32)
     for h in range(halves):
+        if h + 1 < halves:
+            finish_half(h)
+            start_half(h + 1)
         last = filter_half(h, last)
         spread_own(h)
         if h > 0:
@@ -355,13 +369,8 @@
                 arrived(h, lane_of(lax.rem(row + n_row - step, n_row), c, 1 - sub))
     for copy in sends:
         copy.wait_send()
-    for h in range(halves):
-
-        def finish_send(step, carry, h=h):
-            slab(h, step).wait_send()
-            return carry
-
-        lax.fori_loop(1, n, finish_send, 0)
+    finish_half(halves - 1)
+    matrix_copy.wait()
     for step in range(1, n_row):
         weight(step).wait_send()
 
@@ -387,8 +396,9 @@
             jax.ShapeDtypeStruct((beams * 2 * chan, chan * stations2), bf16),
         ),
         in_specs=[any_space] * 6,
-        out_specs=(vmem, vmem),
-        scratch_shapes=[pltpu.VMEM(a.shape, a.dtype) for a in inputs]
+        out_specs=(vmem, any_space),
+        scratch_shapes=[pltpu.VMEM((beams * 2 * chan, chan * stations2), bf16)]
+        + [pltpu.VMEM(a.shape, a.dtype) for a in inputs]
         + [
             pltpu.VMEM((chan, halves, 2, local, width), bf16),
             pltpu.VMEM((halves, 2, n, local, width), bf16),
@@ -400,7 +410,7 @@
             dma((n_row,)), dma((n_row,)), dma((sends,)), dma((halves, n)),
         ],
         compiler_params=pltpu.CompilerParams(
-            collective_id=0, has_side_effects=True, vmem_limit_bytes=24 * 1024 * 1024
+            collective_id=0, has_side_effects=True, vmem_limit_bytes=56 * 1024 * 1024
         ),
         name="exchange",
     )(*inputs)
@@ -441,10 +451,9 @@
     step_index = pl.program_id(0)
     size = out_ref.shape[0]
 
-    def product(index):
-        at = pl.multiple_of(index * size, size)
+    def product():
         return jnp.dot(
-            matrix_ref[pl.ds(at, size), :],
+            matrix_ref[...],
             spectra[...].reshape(chan * stations2, frames),
             preferred_element_type=jnp.float32,
         )
@@ -507,7 +516,7 @@
     stride = 4
     starts = range(0, frames, 128)
 
-    inverse_ref[...] = product(step_index)
+    inverse_ref[...] = product()
     for top in range(0, chan, 8):
         tap_tiles = [wide_taps[tap, top : top + 8, :] for tap in range(taps)]
 
@@ -547,7 +556,11 @@
             jax.ShapeDtypeStruct(vis_shape, jnp.float32),
             jax.ShapeDtypeStruct((matrix.shape[0], frames), jnp.float32),
         ),
-        in_specs=[vmem, vmem, vmem],
+        in_specs=[
+            whole(*lanes.shape),
+            pl.BlockSpec((rows * 2 * chan, matrix.shape[1]), lambda i: (i, 0)),
+            whole(*taps.shape),
+        ],
         out_specs=(
             whole(*vis_shape),
             pl.BlockSpec((rows * 2 * chan, frames), lambda i: (i, 0)),
@@ -559,7 +572,7 @@
             pltpu.VMEM((taps.shape[0], chan, 128), jnp.float32),
         ],
         compiler_params=pltpu.CompilerParams(
-            dimension_semantics=("arbitrary",), vmem_limit_bytes=24 * 1024 * 1024
+            dimension_semantics=("arbitrary",), vmem_limit_bytes=56 * 1024 * 1024
         ),
         name="beamform",
     )(lanes, matrix, taps)

time: 56.4 us -> 53.5 us (0.949)
  local copies, waits for them, and re-layouts: 5.35 us -> 0 us
  Pallas kernels: 50.1 us -> 52.7 us
    unnamed x14 -> x0, local copies, waits for them, and re-layouts: 5.35 us -> none
    pallas_call x1, Pallas kernels: 15.2 us -> 16.7 us  [beamform(): pl.pallas_call(beam_kernel, grid=(beams // rows,), out_shape=(jax.ShapeDt...]
    pallas_call x1, Pallas kernels: 34.9 us -> 36 us  [exchange(): pl.pallas_call(functools.partial(exchange_kernel, n_row, n_col, n_sub), o...]
where the time goes in v4:
time: 53.5 us; the launch traced here: 53.3 us
  Pallas kernels  52.7 us (99%)
  between operations  0.64 us (1%)
    pallas_call x1, Pallas kernels, exchange(): pl.pallas_call(functools.partial(exchange_kernel, n_row, n_col, n_sub), o...  36 us
    pallas_call x1, Pallas kernels, beamform(): pl.pallas_call(beam_kernel, grid=(beams // rows,), out_shape=(jax.ShapeDt...  16.7 us

profile of v4, /device:TPU:0, one launch (start us, length us, event | category | flops | bytes accessed | tf_op | source)
XLA Modules:
  0.0 53.3 jit_solution(16683330402907598984)
XLA Ops:
  0.6 36.0 %exchange.1 = (bf16[2,16,64,256]{3,2,1,0:T(8,128)(2,1)}, bf16[2048,1024]{1,0:T(8,128)(2,1)}) custom-call(bf16[16,2,16,512]{3,2,1,0:T(8,128)(2,1)} %samples_hbm.1, bf16[256,256]{1,0:T(8,128)(2,1)} %bitcast.7, s32[1,256]{1,0:T(1,128)} %bitcast.9, f32[16,16]{1,0:T(8,128)} %taps_hbm.1, s32[1,32]{1,0:T(1,128)} %bitcast.10, s32[8,128]{1,0:T(8,128)} %bitcast.8), custom_call_target="tpu_custom_call" | custom-call | tf_op jit(solution)/shard_map/exchange/pallas_call | solution.py:392
  36.7 16.7 %beamform.1 = (f32[4,2,8,32]{3,2,1,0:T(8,128)}, f32[2048,512]{1,0:T(8,128)}) custom-call(bf16[2,16,64,256]{3,2,1,0:T(8,128)(2,1)} %get-tuple-element.6.lanes_ref, bf16[2048,1024]{1,0:T(8,128)(2,1)} %get-tuple-element.7.matrix_ref, f32[16,16]{1,0:T(8,128)} %taps_ref.1), custom_call_target="tpu_custom_call" | custom-call | tf_op jit(solution)/shard_map/beamform/pallas_call | solution.py:552
